TPU v7x, 1024 devices: a whole 4x4x32 slice. The times are simulated.
1024 devices in a mesh: batch: 128 (over x, z), blk: 8 (over y, core).
Axes of the slice: x: 4, y: 4, z: 32, core: 2. Of those that a mesh axis runs over, the one named last changes fastest.
Arguments:
- basis_values: bfloat16 [128, 2048, 1024], P('batch'), may hold values from -6 to 6
- density: bfloat16 [4096, 128, 128], P(('batch', 'blk')), may hold values from -0.005859375 to 0.005859375
- tile_ids: int32 [128, 32], replicated, may hold values from 0 to 31, as said below
- extra_blocks: int32 [128, 4], P('batch'), may hold values from 0 to 3, as said below
- extra_count: int32 [128], P('batch'), may hold values from 0 to 4, as said below
- point_count: int32 [128], P('batch'), may hold values from 1024 to 2048, as said below
- core_density: float32 [128, 2048], P('batch'), may hold values from 0.5 to 2
- grid_weights: float32 [128, 2048], P('batch'), may hold values from 0.5 to 2
- point_pos: float32 [128, 2048], P('batch'), may hold values from 0 to 1, as said below
- external: float32 [128, 2048], P('batch'), may hold values from -1 to 1
Outputs:
- ham_tiles: float32 [4096, 128, 128], P(('batch', 'blk'))
- potential: float32 [128, 2048], P('batch')
Inputs may be any that keep to these rules, and one draw needn't show every extreme that they name: `tile_ids`: row g names, for the 4 slots of each blk device in turn, the tile each holds; each of the 32 ids appears once in a row, and the first 2 slots of every device hold ids below 16. `extra_blocks`: the 4 entries of a row are different home blocks of group g + 1. `extra_count`: the last group lists none; every other group lists 2 or more; some group lists 4. The first point_count[g] points of group g are live; some group has all 2048. point_pos of group g lies in [g / 128, (g + 1) / 128).
All inputs are finite; a program needn't handle non-finite values.
Results may differ from a plain program's by a relative error of at most 0.0009.
The roundings to bfloat16 on the way count: a program that leaves them out, or rounds other values in their place, can miss the bound.
Values may be sent and summed in bfloat16 or wider, within the bound.
A program may use at most 32 MiB of HBM per device.

v0:
```python
import jax
import jax.numpy as jnp
from jax import lax
from jax.sharding import PartitionSpec as P

NB = 128
HOME = 4
NXT = 4
NMOM = 4


EXCHANGE_COEF = 0.98
HARTREE_SCALE = 0.5


def from_behind(shard, axis, by):
    count = lax.axis_size(axis)
    pairs = [(i, i + by) for i in range(count) if 0 <= i + by < count]
    return lax.ppermute(shard, axis, pairs)


def next_position(block_id, extra_list, extra_num):
    live_slot = jnp.arange(NXT) < extra_num
    matches = (extra_list == block_id) & live_slot
    is_used = jnp.any(matches)
    position = HOME + jnp.sum(jnp.where(matches, jnp.arange(NXT), 0))
    return (is_used, position)


def place_own(tile_id, extra_list, extra_num):
    inner_tile = tile_id < HOME * HOME
    local_id = jnp.where(inner_tile, tile_id, tile_id - HOME * HOME)
    row_block = local_id // HOME
    col_block = local_id % HOME
    col_used, col_pos = next_position(col_block, extra_list, extra_num)
    is_used = inner_tile | col_used
    factor = jnp.where(inner_tile, jnp.float32(1.0), jnp.float32(2.0))
    return (is_used, row_block, jnp.where(inner_tile, col_block, col_pos), factor)


def place_next(tile_id, extra_list, extra_num):
    row_used, row_pos = next_position(tile_id // HOME, extra_list, extra_num)
    col_used, col_pos = next_position(tile_id % HOME, extra_list, extra_num)
    is_used = row_used & col_used & (tile_id < HOME * HOME)
    return (is_used, row_pos, col_pos, jnp.float32(1.0))


def rho_term(basis_vals, tile_data, placed):
    is_used, row_pos, col_pos, factor = placed
    left_cols = lax.dynamic_slice_in_dim(basis_vals, row_pos * NB, NB, 1)
    right_cols = lax.dynamic_slice_in_dim(basis_vals, col_pos * NB, NB, 1)
    product = jnp.dot(left_cols, tile_data, preferred_element_type=jnp.float32)
    return jnp.where(is_used, factor, jnp.float32(0.0)) * jnp.sum(
        product * right_cols.astype(jnp.float32), axis=1
    )


def ham_term(basis_vals, weighted, placed):
    is_used, row_pos, col_pos, factor = placed
    left_cols = lax.dynamic_slice_in_dim(basis_vals, row_pos * NB, NB, 1)
    right_cols = lax.dynamic_slice_in_dim(weighted, col_pos * NB, NB, 1)
    block_sum = lax.dot_general(
        left_cols, right_cols, (((0,), (0,)), ((), ())), preferred_element_type=jnp.float32
    )
    return jnp.where(is_used, jnp.float32(1.0), jnp.float32(0.0)) * block_sum


def sum_rho(basis_vals, tiles, places):

    def sum_one_tile(tile_data, placed):
        return rho_term(basis_vals, tile_data, placed)

    return jnp.sum(jax.vmap(sum_one_tile)(tiles, places), axis=0)


def all_ham(basis_vals, weighted, places):

    def all_one_tile(placed):
        return ham_term(basis_vals, weighted, placed)

    return jax.vmap(all_one_tile)(places)


def body(
    basis_values,
    density,
    tile_ids,
    extra_blocks,
    extra_count,
    point_count,
    core_density,
    grid_weights,
    point_pos,
    external,
):
    group_idx = lax.axis_index("batch")
    member = lax.axis_index("blk")
    groups = lax.axis_size("batch")
    members = lax.axis_size("blk")
    basis_vals = basis_values[0]
    points = basis_vals.shape[0]
    owned = density.shape[0]
    inner_slots = owned // 2
    extra_list = extra_blocks[0]
    extra_num = extra_count[0]
    own_ids = lax.dynamic_slice(tile_ids, (group_idx, member * owned), (1, owned))[0]
    next_group = jnp.minimum(group_idx + 1, groups - 1)
    next_ids = lax.dynamic_slice(tile_ids, (next_group, member * owned), (1, inner_slots))[0]
    arrived = from_behind(density, "batch", -1)[:inner_slots]
    own_places = jax.vmap(lambda tile_id: place_own(tile_id, extra_list, extra_num))(own_ids)
    next_places = jax.vmap(lambda tile_id: place_next(tile_id, extra_list, extra_num))(next_ids)
    rho_part = sum_rho(basis_vals, density, own_places) + sum_rho(basis_vals, arrived, next_places)
    live_mask = (jnp.arange(points) < point_count[0]).astype(jnp.float32)
    coords = point_pos[0]
    powers = jnp.stack([coords**power for power in range(NMOM)])
    weights_row = grid_weights[0]
    core_row = core_density[0]
    total_points = groups * points
    slab_len = points // members
    slab_start = member * slab_len

    def slab(values):
        return lax.dynamic_slice_in_dim(values, slab_start, slab_len, values.ndim - 1)

    delta_rho = lax.psum(rho_part, "blk")
    rho_total = core_row + delta_rho
    moment_terms = (
        jnp.sum(slab(powers) * slab(weights_row * rho_total * live_mask)[None], axis=1)
        / total_points
    )
    moments = lax.psum(moment_terms, ("batch", "blk"))
    far_field = jnp.sum(moments[:, None] * powers, axis=0)
    potential = (
        external[0]
        - EXCHANGE_COEF * rho_total * (1.0 + rho_total * rho_total) ** (-1.0 / 3.0)
        + HARTREE_SCALE * far_field
    )
    quad_weight = weights_row * potential * live_mask / points
    weighted = (quad_weight[:, None] * basis_vals.astype(jnp.float32)).astype(jnp.bfloat16)
    own_ham = all_ham(basis_vals, weighted, own_places)
    lent_ham = all_ham(basis_vals, weighted, next_places)
    padded = jnp.concatenate(
        [lent_ham, jnp.zeros((owned - inner_slots, NB, NB), jnp.float32)], axis=0
    )
    returned = from_behind(padded, "batch", 1)
    ham_tiles = own_ham + returned
    return (ham_tiles, potential[None, :])


def solution(mesh):
    return jax.shard_map(
        body,
        mesh=mesh,
        in_specs=(
            P("batch", None, None),
            P(("batch", "blk"), None, None),
            P(),
            P("batch", None),
            P("batch"),
            P("batch"),
            P("batch", None),
            P("batch", None),
            P("batch", None),
            P("batch", None),
        ),
        out_specs=(P(("batch", "blk"), None, None), P("batch", None)),
        check_vma=False,
    )
```

profile of v0, /device:TPU:1, one launch (start us, length us, event | category | flops | bytes accessed | tf_op | source)
XLA Modules:
  0.0 268.2 jit_solution(8511979758832731283)
XLA Ops:
  0.6 1.0 copy.24
  1.7 1.3 collective-permute-start
  3.9 0.8 select_reduce_fusion
  4.7 0.8 fusion.3
  5.8 0.9 fusion.8
  6.6 0.9 fusion.7
  7.9 5.3 %while.8 = (s32[]{:T(128)}, bf16[2048,1024]{1,0:T(8,128)(2,1)}, s32[2,2]{1,0:T(2,128)S(1)}, bf16[2,2048,128]{2,1,0:T(8,128)(2,1)S(1)}, s32[]{:T(128)}) while((s32[]{:T(128)}, bf16[2048,1024]{1,0:T(8,128)(2,1)}, s32[2,2]{1,0:T(2,128)S(1)}, bf16[2,2048,128]{2,1,0:T(8,128)(2,1)S(1)}, s32[]{:T(128)}) %tuple.107), condition=%wide.while_cond.2, body=%wide.while_body.2.sunk | while | flops 2 | bytes 1048681 | solution.py:50
  7.9 0.6 slice.81
  8.4 2.1 bitcast_dynamic-update-slice_fusion.9
  10.5 0.6 slice.81
  11.1 2.1 bitcast_dynamic-update-slice_fusion.9
  14.1 15.0 %while.7 = (s32[]{:T(128)}, bf16[2048,1024]{1,0:T(8,128)(2,1)}, s32[4,2]{0,1:T(2,128)S(1)}, bf16[4,2048,128]{1,2,0:T(8,128)(2,1)}, s32[]{:T(128)}) while((s32[]{:T(128)}, bf16[2048,1024]{1,0:T(8,128)(2,1)}, s32[4,2]{0,1:T(2,128)S(1)}, bf16[4,2048,128]{1,2,0:T(8,128)(2,1)}, s32[]{:T(128)}) %tuple.108), condition=%wide.while_cond.1, body=%wide.while_body.1.sunk | while | flops 2 | bytes 3145833 | solution.py:51
  14.2 0.5 slice.80
  14.7 2.1 dynamic-slice_bitcast_fusion.4
  17.1 0.8 constant_dynamic-update-slice_fusion.4
  18.0 0.5 slice.80
  18.5 2.1 dynamic-slice_bitcast_fusion.4
  20.8 0.8 constant_dynamic-update-slice_fusion.4
  21.7 0.5 slice.80
  22.2 2.1 dynamic-slice_bitcast_fusion.4
  24.6 0.9 constant_dynamic-update-slice_fusion.4
  25.5 0.5 slice.80
  26.0 2.1 dynamic-slice_bitcast_fusion.4
  28.3 0.9 constant_dynamic-update-slice_fusion.4
  29.5 11.1 %while.6 = (s32[]{:T(128)}, bf16[2048,1024]{1,0:T(8,128)(2,1)}, s32[4,2]{0,1:T(2,128)S(1)}, bf16[4,2048,128]{2,1,0:T(8,128)(2,1)S(1)}, s32[]{:T(128)}) while((s32[]{:T(128)}, bf16[2048,1024]{1,0:T(8,128)(2,1)}, s32[4,2]{0,1:T(2,128)S(1)}, bf16[4,2048,128]{2,1,0:T(8,128)(2,1)S(1)}, s32[]{:T(128)}) %tuple.109), condition=%wide.while_cond, body=%wide.while_body.sunk | while | flops 2 | bytes 1048681 | solution.py:60
  29.5 0.5 slice.79
  30.1 2.2 bitcast_dynamic-update-slice_fusion.8
  32.3 0.5 slice.79
  32.8 2.2 bitcast_dynamic-update-slice_fusion.8
  35.1 0.5 slice.79
  35.6 2.2 bitcast_dynamic-update-slice_fusion.8
  37.8 0.5 slice.79
  38.4 2.2 bitcast_dynamic-update-slice_fusion.8
  40.7 7.5 %while.9 = (s32[]{:T(128)}, bf16[2048,1024]{1,0:T(8,128)(2,1)}, s32[2,2]{1,0:T(2,128)S(1)}, bf16[2,2048,128]{1,2,0:T(8,128)(2,1)}, s32[]{:T(128)}) while((s32[]{:T(128)}, bf16[2048,1024]{1,0:T(8,128)(2,1)}, s32[2,2]{1,0:T(2,128)S(1)}, bf16[2,2048,128]{1,2,0:T(8,128)(2,1)}, s32[]{:T(128)}) %tuple.110), condition=%wide.while_cond.3, body=%wide.while_body.3.sunk | while | flops 2 | bytes 3145833 | solution.py:51
  40.7 0.6 slice.82
  41.3 2.1 dynamic-slice_bitcast_fusion.5
  43.6 0.8 constant_dynamic-update-slice_fusion.5
  44.5 0.6 slice.82
  45.1 2.1 dynamic-slice_bitcast_fusion.5
  47.4 0.9 constant_dynamic-update-slice_fusion.5
  48.3 2.5 multiply_reduce_fusion
  51.0 1.7 fusion
  52.8 26.1 %psum.14 = f32[2048]{0:T(1024)S(1)} all-reduce(f32[2048]{0:T(1024)S(1)} %add.199), channel_id=1, replica_groups=mesh['batch'=128,'blk'=8] {'blk'}, use_global_device_ids=true, to_apply=%region_10.11 | all-reduce | flops 2048 | bytes 16384 | tf_op jit(solution)/shard_map/psum | solution.py:125
  79.2 159.0 %psum.15 = f32[4]{0:T(128)S(1)} all-reduce(f32[4]{0:T(128)S(1)} %broadcast_multiply_fusion), channel_id=1, replica_groups=mesh['batch'=128,'blk'=8] {'batch','blk'}, use_global_device_ids=true, to_apply=%region_12.13 | all-reduce | flops 4 | bytes 32 | tf_op jit(solution)/shard_map/psum | solution.py:131
  238.3 0.6 select_multiply_fusion
  239.0 4.9 %multiply_convert_fusion = bf16[2048,1024]{1,0:T(8,128)(2,1)} fusion(f32[2048]{0:T(1024)S(1)} %get-tuple-element.126, bf16[1,2048,1024]{2,1,0:T(8,128)(2,1)} %bitcast.84), kind=kLoop, calls=%fused_computation.14 | loop fusion | flops 6291456 | bytes 8396800 | tf_op jit(solution)/shard_map/convert_element_type | solution.py:139
  244.0 5.6 %while.11 = (s32[]{:T(128)}, bf16[2048,1024]{1,0:T(8,128)(2,1)}, s32[2,2]{1,0:T(2,128)S(1)}, bf16[2,2048,128]{2,1,0:T(8,128)(2,1)S(1)}, s32[]{:T(128)}) while((s32[]{:T(128)}, bf16[2048,1024]{1,0:T(8,128)(2,1)}, s32[2,2]{1,0:T(2,128)S(1)}, bf16[2,2048,128]{2,1,0:T(8,128)(2,1)S(1)}, s32[]{:T(128)}) %tuple.113), condition=%wide.while_cond.5, body=%wide.while_body.5.sunk | while | flops 2 | bytes 1048681 | solution.py:61
  244.0 0.6 slice.84
  244.6 2.1 bitcast_dynamic-update-slice_fusion.11
  246.8 0.6 slice.84
  247.4 2.1 bitcast_dynamic-update-slice_fusion.11
  249.5 0.5 convolution_multiply_fusion.2
  250.1 3.6 %collective-permute-start.1 = (f32[4,128,128]{2,1,0:T(8,128)S(1)}, f32[4,128,128]{2,1,0:T(8,128)S(1)}, u32[]{:S(2)}, u32[]{:S(2)}) collective-permute-start(f32[4,128,128]{2,1,0:T(8,128)S(1)} %concatenate.23), channel_id=1, source_target_pairs={{0,8},{8,16},{16,24},{24,32},{32,40},{40,48},{48,56},{56,64},{64,7... | collective-permute-start | bytes 786440 | tf_op jit(solution)/shard_map/ppermute | solution.py:19
  253.6 0.3 broadcast.434
  253.9 11.1 %while.10 = (s32[]{:T(128)}, bf16[2048,1024]{1,0:T(8,128)(2,1)}, s32[4,2]{0,1:T(2,128)S(1)}, bf16[4,2048,128]{2,1,0:T(8,128)(2,1)S(1)}, s32[]{:T(128)}) while((s32[]{:T(128)}, bf16[2048,1024]{1,0:T(8,128)(2,1)}, s32[4,2]{0,1:T(2,128)S(1)}, bf16[4,2048,128]{2,1,0:T(8,128)(2,1)S(1)}, s32[]{:T(128)}) %tuple.112), condition=%wide.while_cond.4, body=%wide.while_body.4.sunk | while | flops 2 | bytes 1048681 | solution.py:61
  254.0 0.5 slice.83
  254.5 2.2 bitcast_dynamic-update-slice_fusion.10
  256.8 0.5 slice.83
  257.3 2.2 bitcast_dynamic-update-slice_fusion.10
  259.5 0.5 slice.83
  260.1 2.2 bitcast_dynamic-update-slice_fusion.10
  262.3 0.5 slice.83
  262.8 2.2 bitcast_dynamic-update-slice_fusion.10
  265.0 3.2 %fusion.1 = f32[4,128,128]{2,1,0:T(8,128)} fusion(f32[4,128,128]{2,1,0:T(8,128)S(1)} %collective-permute-done.1, bf16[4,2048,128]{2,1,0:T(8,128)(2,1)} %copy-done.1, bf16[4,2048,128]{2,1,0:T(8,128)(2,1)S(1)} %get-tuple-element.41, f32[4]{0:T(128)S(1)} %get-tuple-element.130), kind=kOutput, calls=%fused_computation.19 | convolution fusion | flops 268566528 | bytes 4718608 | tf_op jit(solution)/shard_map/vmap()/dot_general | solution.py:62
  (77 shorter events, 4.5 us)
Async XLA Ops:
  0.6 3.0 %copy-start = (s32[128,32]{0,1:T(8,128)S(1)}, s32[128,32]{0,1:T(8,128)}, u32[]{:S(2)}) copy-start(s32[128,32]{0,1:T(8,128)} %param.12) | copy-start | bytes 49156
  1.7 49.3 %collective-permute-start = (bf16[4,128,128]{1,2,0:T(8,128)(2,1)S(1)}, bf16[4,128,128]{1,2,0:T(8,128)(2,1)}, u32[]{:S(2)}, u32[]{:S(2)}) collective-permute-start(bf16[4,128,128]{1,2,0:T(8,128)(2,1)S(1)} %copy.24), channel_id=1, source_target_pairs={{8,0},{16,8},{24,16},{32,24},{40,32},{48,40},{56,48},{64,56},{72,6... | collective-permute-start | bytes 393224 | tf_op jit(solution)/shard_map/ppermute | solution.py:19
  7.8 6.0 %copy-start.5 = (f32[1,2048]{1,0:T(1,128)S(1)}, f32[1,2048]{1,0:T(1,128)}, u32[]{:S(2)}) copy-start(f32[1,2048]{1,0:T(1,128)} %param.18) | copy-start | bytes 24580
  13.2 1.0 copy-start.2
  40.5 7.7 %copy-start.1 = (bf16[4,2048,128]{2,1,0:T(8,128)(2,1)}, bf16[4,2048,128]{2,1,0:T(8,128)(2,1)S(1)}, u32[]{:S(2)}) copy-start(bf16[4,2048,128]{2,1,0:T(8,128)(2,1)S(1)} %get-tuple-element.9) | copy-start | bytes 6291460
  40.7 7.5 %copy-start.4 = (bf16[4,128,128]{2,1,0:T(8,128)(2,1)S(1)}, bf16[4,128,128]{2,1,0:T(8,128)(2,1)}, u32[]{:S(2)}) copy-start(bf16[4,128,128]{2,1,0:T(8,128)(2,1)} %param.11) | copy-start | bytes 393220
  48.3 2.7 %copy-start.3 = (bf16[2,2048,128]{2,1,0:T(8,128)(2,1)S(1)}, bf16[2,2048,128]{2,1,0:T(8,128)(2,1)}, u32[]{:S(2)}) copy-start(bf16[2,2048,128]{2,1,0:T(8,128)(2,1)} %copy-done.2) | copy-start | bytes 3145732
  50.7 28.3 %copy-start.7 = (f32[1,2048]{1,0:T(1,128)S(1)}, f32[1,2048]{1,0:T(1,128)}, u32[]{:S(2)}) copy-start(f32[1,2048]{1,0:T(1,128)} %param.16) | copy-start | bytes 24580
  50.7 28.3 %copy-start.6 = (f32[1,2048]{1,0:T(1,128)S(1)}, f32[1,2048]{1,0:T(1,128)}, u32[]{:S(2)}) copy-start(f32[1,2048]{1,0:T(1,128)} %param.17) | copy-start | bytes 24580
  50.7 187.6 %copy-start.8 = (f32[1,2048]{1,0:T(1,128)S(1)}, f32[1,2048]{1,0:T(1,128)}, u32[]{:S(2)}) copy-start(f32[1,2048]{1,0:T(1,128)} %param.19) | copy-start | bytes 24580
  250.1 14.9 %collective-permute-start.1 = (f32[4,128,128]{2,1,0:T(8,128)S(1)}, f32[4,128,128]{2,1,0:T(8,128)S(1)}, u32[]{:S(2)}, u32[]{:S(2)}) collective-permute-start(f32[4,128,128]{2,1,0:T(8,128)S(1)} %concatenate.23), channel_id=1, source_target_pairs={{0,8},{8,16},{16,24},{24,32},{32,40},{40,48},{48,56},{56,64},{64,7... | collective-permute-start | bytes 786440 | tf_op jit(solution)/shard_map/ppermute | solution.py:19
where the time goes:
time: 270 us; the launch traced here: 268 us
  blocking collectives  185 us (69%)
  local copies, waits for them, and re-layouts  58.1 us (22%)
  other arithmetic  9.59 us (4%)
  matrix products  7.88 us (3%)
  starting transfers between devices  4.84 us (2%)
    psum x1, blocking collectives, body(): moments = lax.psum(moment_terms, ('batch', 'blk'))  159 us
    gather x66, local copies, waits for them, and re-layouts  55.2 us
    psum x1, blocking collectives, body(): delta_rho = lax.psum(rho_part, 'blk')  26.1 us
  transfers between devices with their start and end apart: 2, of which 0 were waited for; matrix products, arithmetic and copies ran while one was open for 21% of the time, Pallas kernels for 0%

commit v1 on v0

v1 whole, which is shorter than its diff:
```python
import functools

import jax
import jax.numpy as jnp
from jax import lax
from jax.experimental import pallas as pl
from jax.experimental.pallas import tpu as pltpu
from jax.sharding import PartitionSpec as P

NB = 128
HOME = 4
NXT = 4
NMOM = 4
Z_LEN = 32
CHUNK = 256
LOADS = 4

EXCHANGE_COEF = 0.98
HARTREE_SCALE = 0.5
MESH = pl.DeviceIdType.MESH
F32 = jnp.float32
BF16 = jnp.bfloat16


def next_position(block_id, extra_list, extra_num):
    used = jnp.int32(0)
    position = jnp.int32(0)
    for slot in range(NXT):
        match = jnp.where((extra_list[slot] == block_id) & (slot < extra_num), 1, 0)
        used = used + match
        position = position + match * slot
    return used, position


def place_inner(tile_id, extra_list, extra_num):
    return jnp.int32(1), lax.div(tile_id, HOME), lax.rem(tile_id, HOME), jnp.int32(1)


def place_cross(tile_id, extra_list, extra_num):
    local_id = tile_id - HOME * HOME
    used, position = next_position(lax.rem(local_id, HOME), extra_list, extra_num)
    return used, lax.div(local_id, HOME), position, used * 2


def place_next(tile_id, extra_list, extra_num):
    row_used, row_pos = next_position(lax.div(tile_id, HOME), extra_list, extra_num)
    col_used, col_pos = next_position(lax.rem(tile_id, HOME), extra_list, extra_num)
    is_used = row_used * col_used
    return is_used, row_pos, col_pos, is_used


def pick(ref, span, first, number):
    blocks = [ref[span, (first + b) * NB : (first + b + 1) * NB] for b in range(HOME)]
    out = blocks[0]
    for b in range(1, HOME):
        out = jnp.where(number == b, blocks[b], out)
    return out


def kernel(
    sizes,
    ids_ref, extra_ref, count_ref, live_ref,
    basis_hbm, density_hbm, core_hbm, weight_hbm, pos_hbm, ext_hbm,
    ham_ref, pot_ref,
    basis, left, flipped, tiles, arrived, core_row, weight_row, pos_row, ext_row,
    acc, rho_own, rho_slots, mom_row, mom_slots, part_row, part_slots,
    weighted, quad, lent, returned,
    load_sem, small_sem, den_sem, rho_sem, mom_sem, part_sem, lent_sem,
):
    groups, members, z_len, points = sizes
    x_len = groups // z_len
    plane = x_len * members
    rows = points // NB
    owned = density_hbm.shape[0]
    inner_slots = owned // 2

    g = lax.axis_index("batch")
    m = lax.axis_index("blk")
    x = lax.div(g, z_len)
    z = lax.rem(g, z_len)
    here = x * members + m
    up = (lax.rem(g + 1, groups), m)
    down = (lax.rem(g + groups - 1, groups), m)

    def along_z(step):
        return (x * z_len + lax.rem(z + step, z_len), m)

    def in_plane(step):
        there = lax.rem(here + step, plane)
        return (lax.div(there, members) * z_len + z, lax.rem(there, members))

    def in_group(step):
        return (g, lax.rem(m + step, members))

    part = points // LOADS
    loads = []
    for i in range(LOADS):
        span = pl.ds(i * part, part)
        loads.append(pltpu.make_async_copy(basis_hbm.at[0, span], basis.at[span], load_sem.at[i]))
    small = [
        pltpu.make_async_copy(src, dst, small_sem.at[i])
        for i, (src, dst) in enumerate(
            [
                (density_hbm, tiles),
                (core_hbm, core_row),
                (weight_hbm, weight_row),
                (pos_hbm, pos_row),
                (ext_hbm, ext_row),
            ]
        )
    ]

    barrier = pltpu.get_barrier_semaphore()
    for neighbour in (up, down):
        pl.semaphore_signal(barrier, inc=1, device_id=neighbour, device_id_type=MESH)

    def greet_plane(step, carry):
        pl.semaphore_signal(barrier, inc=1, device_id=in_plane(step), device_id_type=MESH)
        return carry

    def greet_z(step, carry):
        pl.semaphore_signal(barrier, inc=1, device_id=along_z(step), device_id_type=MESH)
        return carry

    lax.fori_loop(1, z_len, greet_z, 0)
    lax.fori_loop(1, plane, greet_plane, 0)
    small[0].start()
    for copy in loads:
        copy.start()
    for copy in small[1:]:
        copy.start()

    extra_list = [extra_ref[0, slot] for slot in range(NXT)]
    extra_num = count_ref[0]
    g_up = lax.rem(g + 1, groups)
    own_places = [
        (place_inner if s < inner_slots else place_cross)(
            ids_ref[g, m * owned + s], extra_list, extra_num
        )
        for s in range(owned)
    ]
    next_places = [
        place_next(ids_ref[g_up, m * owned + s], extra_list, extra_num)
        for s in range(inner_slots)
    ]

    pl.semaphore_wait(barrier, (z_len - 1) + (plane - 1) + 2)

    density_copy = pltpu.make_async_remote_copy(
        src_ref=density_hbm.at[pl.ds(0, inner_slots)],
        dst_ref=arrived,
        send_sem=den_sem.at[0],
        recv_sem=den_sem.at[1],
        device_id=down,
        device_id_type=MESH,
    )
    density_copy.start()

    small[0].wait()
    for s in range(owned):
        factor = own_places[s][3].astype(F32)
        tiles[s] = (tiles[s].astype(F32) * factor).astype(BF16)

    places = own_places + next_places
    firsts = [(0, 0)] * inner_slots + [(0, HOME)] * (owned - inner_slots)
    firsts = firsts + [(HOME, HOME)] * inner_slots

    def tile_terms(span, stack, slots):
        total = None
        for i, s in enumerate(slots):
            _, row, col, _ = places[s]
            block = pick(basis, span, firsts[s][0], row)
            left[s, span, :] = block
            product = jnp.dot(block, stack[i], preferred_element_type=F32)
            term = product * pick(basis, span, firsts[s][1], col).astype(F32)
            total = term if total is None else total + term
        return total

    for i in range(LOADS):
        loads[i].wait()

    def own_chunk(c, carry):
        span = pl.ds(pl.multiple_of(c * CHUNK, CHUNK), CHUNK)
        acc[span, :] = tile_terms(span, tiles, range(owned))
        return carry

    lax.fori_loop(0, points // CHUNK, own_chunk, 0)
    for copy in small[1:]:
        copy.wait()

    density_copy.wait()
    for s in range(inner_slots):
        factor = next_places[s][3].astype(F32)
        arrived[s] = (arrived[s].astype(F32) * factor).astype(BF16)

    def next_chunk(c, carry):
        span = pl.ds(pl.multiple_of(c * CHUNK, CHUNK), CHUNK)
        total = acc[span, :] + tile_terms(span, arrived, range(owned, len(places)))
        for i in range(CHUNK // NB):
            turned = total[i * NB : (i + 1) * NB].T
            rho_own[pl.ds(c * (CHUNK // NB) + i, 1), :] = jnp.sum(turned, axis=0, keepdims=True)
        return carry

    lax.fori_loop(0, points // CHUNK, next_chunk, 0)

    rho_part = rho_own[...]
    pos = pos_row[...]
    index = lax.broadcasted_iota(jnp.int32, (rows, NB), 0) * NB + lax.broadcasted_iota(
        jnp.int32, (rows, NB), 1
    )
    live = jnp.where(index < live_ref[0], F32(1.0), F32(0.0))
    live_weight = weight_row[...] * live
    core_share = jnp.where(m == 0, F32(1.0), F32(0.0))
    term = live_weight * (rho_part + core_row[...] * core_share) * F32(1.0 / (groups * points))
    sums = []
    for power in range(NMOM):
        sums.append(jnp.sum(term, axis=0, keepdims=True))
        term = term * pos
    stack = jnp.concatenate(sums + [jnp.zeros((8 - NMOM, NB), F32)], axis=0)
    width = NB // NMOM
    stack = stack + pltpu.roll(stack, NB // 2, 1)
    stack = stack + pltpu.roll(stack, NB // 4, 1)
    quarter = lax.div(lax.broadcasted_iota(jnp.int32, (8, NB), 1), width)
    keep = quarter == lax.broadcasted_iota(jnp.int32, (8, NB), 0)
    row = jnp.sum(jnp.where(keep, stack, F32(0.0)), axis=0, keepdims=True)
    mom_row[...] = row
    mom_slots[z] = row

    def mom_copy(step):
        return pltpu.make_async_remote_copy(
            src_ref=mom_row,
            dst_ref=mom_slots.at[z],
            send_sem=mom_sem.at[0],
            recv_sem=mom_sem.at[1],
            device_id=along_z(step),
            device_id_type=MESH,
        )

    def send_mom(i, carry):
        step = z_len // 2 + lax.div(i + 1, 2) * (1 - 2 * lax.rem(i, 2))
        mom_copy(step).start()
        return carry

    lax.fori_loop(0, z_len - 1, send_mom, 0)

    rho_slots[m] = rho_part

    def rho_copy(step):
        return pltpu.make_async_remote_copy(
            src_ref=rho_own,
            dst_ref=rho_slots.at[m],
            send_sem=rho_sem.at[0],
            recv_sem=rho_sem.at[1],
            device_id=in_group(step),
            device_id_type=MESH,
        )

    def send_rho(step, carry):
        rho_copy(step).start()
        return carry

    lax.fori_loop(1, members, send_rho, 0)

    def flip_chunk(c, carry):
        span = pl.ds(pl.multiple_of(c * NB, NB), NB)
        for s, (_, _, col, _) in enumerate(places):
            flipped[s, :, span] = pick(basis, span, firsts[s][1], col).T
        return carry

    lax.fori_loop(0, rows, flip_chunk, 0)

    def wait_all(slots, count, sem, target):
        both = pltpu.make_async_remote_copy(
            src_ref=slots.at[pl.ds(0, count)],
            dst_ref=slots.at[pl.ds(0, count)],
            send_sem=sem.at[0],
            recv_sem=sem.at[1],
            device_id=target,
            device_id_type=MESH,
        )
        return both

    mom_all = wait_all(mom_slots, z_len - 1, mom_sem, along_z(1))
    mom_all.wait_recv()
    column = jnp.sum(mom_slots[...], axis=0)
    part_row[...] = column
    part_slots[here] = column

    def part_copy(step):
        return pltpu.make_async_remote_copy(
            src_ref=part_row,
            dst_ref=part_slots.at[here],
            send_sem=part_sem.at[0],
            recv_sem=part_sem.at[1],
            device_id=in_plane(step),
            device_id_type=MESH,
        )

    def send_part(step, carry):
        part_copy(step).start()
        return carry

    lax.fori_loop(1, plane, send_part, 0)

    rho_all = wait_all(rho_slots, members - 1, rho_sem, in_group(1))
    rho_all.wait_recv()
    rho = core_row[...] + jnp.sum(rho_slots[...], axis=0)
    local = ext_row[...] - F32(EXCHANGE_COEF) * rho * jnp.exp(
        F32(-1.0 / 3.0) * jnp.log(F32(1.0) + rho * rho)
    )
    scaled_weight = live_weight * F32(1.0 / points)

    part_all = wait_all(part_slots, plane - 1, part_sem, in_plane(1))
    part_all.wait_recv()
    total = jnp.sum(part_slots[...], axis=0)
    lane = lax.div(lax.broadcasted_iota(jnp.int32, (1, NB), 1), width)
    moments = [
        jnp.sum(jnp.where(lane == power, total, F32(0.0)), axis=1, keepdims=True)
        for power in range(NMOM)
    ]
    far = moments[3]
    for power in (2, 1, 0):
        far = far * pos + moments[power]
    potential = local + F32(HARTREE_SCALE) * far
    pot_ref[...] = potential
    quad[...] = scaled_weight * potential

    def ham_tile(s):
        for i in range(rows):
            span = slice(i * NB, (i + 1) * NB)
            block = flipped[s, :, span].astype(F32)
            weighted[:, span] = (block * quad[i : i + 1, :]).astype(BF16)
        turned = jnp.dot(weighted[...], left[s], preferred_element_type=F32)
        return turned.T * places[s][0].astype(F32)

    lent_copies = []
    for s in range(inner_slots):
        lent[s] = ham_tile(owned + s)
        copy = pltpu.make_async_remote_copy(
            src_ref=lent.at[s],
            dst_ref=returned.at[s],
            send_sem=lent_sem.at[0, s],
            recv_sem=lent_sem.at[1, s],
            device_id=up,
            device_id_type=MESH,
        )
        copy.start()
        lent_copies.append(copy)
    for s in range(owned):
        ham_ref[s] = ham_tile(s)
    for s in range(inner_slots):
        lent_copies[s].wait()
        ham_ref[s] = ham_ref[s] + returned[s]

    mom_all.wait_send()
    rho_all.wait_send()
    part_all.wait_send()


def body(
    basis_values, density, tile_ids, extra_blocks, extra_count, point_count,
    core_density, grid_weights, point_pos, external,
):
    groups = lax.axis_size("batch")
    members = lax.axis_size("blk")
    points = basis_values.shape[1]
    owned = density.shape[0]
    inner_slots = owned // 2
    rows = points // NB
    columns = basis_values.shape[2]
    z_len = min(Z_LEN, groups)
    plane = groups // z_len * members
    smem = pl.BlockSpec(memory_space=pltpu.SMEM)
    anywhere = pl.BlockSpec(memory_space=pl.ANY)
    vmem = pl.BlockSpec(memory_space=pltpu.VMEM)
    ham_tiles, potential = pl.pallas_call(
        functools.partial(kernel, (groups, members, z_len, points)),
        out_shape=(
            jax.ShapeDtypeStruct((owned, NB, NB), F32),
            jax.ShapeDtypeStruct((rows, NB), F32),
        ),
        in_specs=[smem] * 4 + [anywhere] * 6,
        out_specs=(vmem, vmem),
        scratch_shapes=[
            pltpu.VMEM((points, columns), BF16),
            pltpu.VMEM((owned + inner_slots, points, NB), BF16),
            pltpu.VMEM((owned + inner_slots, NB, points), BF16),
            pltpu.VMEM((owned, NB, NB), BF16),
            pltpu.VMEM((inner_slots, NB, NB), BF16),
            pltpu.VMEM((rows, NB), F32),
            pltpu.VMEM((rows, NB), F32),
            pltpu.VMEM((rows, NB), F32),
            pltpu.VMEM((rows, NB), F32),
            pltpu.VMEM((points, NB), F32),
            pltpu.VMEM((rows, NB), F32),
            pltpu.VMEM((members, rows, NB), F32),
            pltpu.VMEM((1, NB), F32),
            pltpu.VMEM((z_len, 1, NB), F32),
            pltpu.VMEM((1, NB), F32),
            pltpu.VMEM((plane, 1, NB), F32),
            pltpu.VMEM((NB, points), BF16),
            pltpu.VMEM((rows, NB), F32),
            pltpu.VMEM((inner_slots, NB, NB), F32),
            pltpu.VMEM((inner_slots, NB, NB), F32),
            pltpu.SemaphoreType.DMA((LOADS,)),
            pltpu.SemaphoreType.DMA((5,)),
            pltpu.SemaphoreType.DMA((2,)),
            pltpu.SemaphoreType.DMA((2,)),
            pltpu.SemaphoreType.DMA((2,)),
            pltpu.SemaphoreType.DMA((2,)),
            pltpu.SemaphoreType.DMA((2, inner_slots)),
        ],
        compiler_params=pltpu.CompilerParams(
            collective_id=0, has_side_effects=True, vmem_limit_bytes=40 * 1024 * 1024
        ),
        name="density_hamiltonian",
    )(
        tile_ids, extra_blocks, extra_count, point_count,
        basis_values, density,
        core_density.reshape(rows, NB), grid_weights.reshape(rows, NB),
        point_pos.reshape(rows, NB), external.reshape(rows, NB),
    )
    return ham_tiles, potential.reshape(1, points)


def solution(mesh):
    return jax.shard_map(
        body,
        mesh=mesh,
        in_specs=(
            P("batch", None, None),
            P(("batch", "blk"), None, None),
            P(),
            P("batch", None),
            P("batch"),
            P("batch"),
            P("batch", None),
            P("batch", None),
            P("batch", None),
            P("batch", None),
        ),
        out_specs=(P(("batch", "blk"), None, None), P("batch", None)),
        check_vma=False,
    )
```

time: 270 us -> 70 us (0.26)
  blocking collectives: 185 us -> 0 us
  Pallas kernels: 0 us -> 58.9 us
  local copies, waits for them, and re-layouts: 58.1 us -> 8.65 us
  other arithmetic: 9.59 us -> 0 us
  matrix products: 7.88 us -> 0 us
  starting transfers between devices: 4.84 us -> 0 us
    psum x2 -> x0, blocking collectives: 185 us -> none  [the longest x1 159 us: body(): moments = lax.psum(moment_terms, ('batch', 'blk'))]
    pallas_call x0 -> x1, Pallas kernels: none -> 58.9 us  [body(): pl.pallas_call(functools.partial(kernel, (groups, members, z_len, points)...]
    gather x66 -> x0, local copies, waits for them, and re-layouts: 55.2 us -> none
    dot_general x4 -> x0, matrix products: 7.88 us -> none  [the longest x2 4.17 us: rho_term(): product = jnp.dot(left_cols, tile_data, preferred_element_type=jnp.float32)]
    unnamed x25 -> x17, local copies, waits for them, and re-layouts: 2.34 us -> 8.65 us
    convert_element_type x1 -> x0, other arithmetic: 4.86 us -> none  [body(): (quad_weight[:, None] * basis_vals.astype(jnp.float32)).astype(jnp.bfloat16)]
    ppermute x2 -> x0, starting transfers between devices: 4.84 us -> none  [from_behind(): return lax.ppermute(shard, axis, pairs)]
  transfers between devices with their start and end apart: 2 -> 0, of which waited for: 0 -> 0; matrix products, arithmetic and copies ran while one was open for 21% -> 0% of each run, Pallas kernels for 0% -> 0%
where the time goes in v1:
time: 70 us; the launch traced here: 69.5 us
  Pallas kernels  58.9 us (84%)
  local copies, waits for them, and re-layouts  8.65 us (12%)
  between operations  1.95 us (3%)
    pallas_call x1, Pallas kernels, body(): pl.pallas_call(functools.partial(kernel, (groups, members, z_len, points)...  58.9 us
    unnamed x17, local copies, waits for them, and re-layouts  8.65 us

profile of v1, /device:TPU:1, one launch (start us, length us, event | category | flops | bytes accessed | tf_op | source)
XLA Modules:
  0.0 69.5 jit_solution(2728493027809187032)
XLA Ops:
  1.9 0.8 %copy.12.ids_ref = s32[128,32]{1,0:T(8,128)S(1)} copy(s32[128,32]{0,1:T(8,128)} %param.12) | data formatting | bytes 32768 | tf_op args[2]
  2.7 0.0 copy-start
  2.7 2.2 %copy-done = bf16[1,2048,1024]{2,1,0:T(8,128)(2,1)S(1)} copy-done((bf16[1,2048,1024]{2,1,0:T(8,128)(2,1)S(1)}, bf16[1,2048,1024]{2,1,0:T(8,128)(2,1)}, u32[]{:S(2)}) %copy-start) | copy-done | bytes 4194328
  4.9 0.0 copy-start.1
  4.9 0.9 %copy-done.1 = bf16[4,128,128]{2,1,0:T(8,128)(2,1)S(1)} copy-done((bf16[4,128,128]{2,1,0:T(8,128)(2,1)S(1)}, bf16[4,128,128]{2,1,0:T(8,128)(2,1)}, u32[]{:S(2)}) %copy-start.1) | copy-done | bytes 131096
  5.8 0.0 copy-start.2
  5.8 0.7 copy-done.2
  6.5 0.0 copy-start.3
  6.5 0.7 copy-done.3
  7.2 0.0 copy-start.4
  7.2 0.7 copy-done.4
  7.9 0.0 copy-start.5
  7.9 0.7 copy-done.5
  8.6 0.0 copy-start.6
  8.6 0.7 copy-done.6
  9.3 58.9 %density_hamiltonian.1 = (f32[4,128,128]{2,1,0:T(8,128)S(1)}, f32[16,128]{1,0:T(8,128)S(1)}) custom-call(s32[128,32]{1,0:T(8,128)S(1)} %copy.12.ids_ref, s32[1,4]{1,0:T(1,128)S(1)} %copy-done.6, s32[1]{0:T(128)S(6)} %copy.15.count_ref, s32[1]{0:T(128)S(6)} %copy.16.live_ref, bf16[1,2048,1024]{2,1,0:T(8,128)(2,1)S(1)} %copy-done, ...), custom_call_target="tpu_custom_call" | custom-call | tf_op jit(solution)/shard_map/density_hamiltonian/pallas_call | solution.py:376
  68.2 0.7 %copy.17 = f32[4,128,128]{2,1,0:T(8,128)} copy(f32[4,128,128]{2,1,0:T(8,128)S(1)} %get-tuple-element.8) | data formatting | bytes 524288
  68.9 0.6 copy.18
Async XLA Ops:
  2.7 2.2 %copy-start = (bf16[1,2048,1024]{2,1,0:T(8,128)(2,1)S(1)}, bf16[1,2048,1024]{2,1,0:T(8,128)(2,1)}, u32[]{:S(2)}) copy-start(bf16[1,2048,1024]{2,1,0:T(8,128)(2,1)} %basis_hbm.1) | copy-start | bytes 12582916
  4.9 0.9 %copy-start.1 = (bf16[4,128,128]{2,1,0:T(8,128)(2,1)S(1)}, bf16[4,128,128]{2,1,0:T(8,128)(2,1)}, u32[]{:S(2)}) copy-start(bf16[4,128,128]{2,1,0:T(8,128)(2,1)} %density_hbm.1) | copy-start | bytes 393220
  5.8 0.7 %copy-start.2 = (f32[1,2048]{1,0:T(1,128)S(1)}, f32[1,2048]{1,0:T(1,128)}, u32[]{:S(2)}) copy-start(f32[1,2048]{1,0:T(1,128)} %param.16) | copy-start | bytes 24580
  6.5 0.7 %copy-start.3 = (f32[1,2048]{1,0:T(1,128)S(1)}, f32[1,2048]{1,0:T(1,128)}, u32[]{:S(2)}) copy-start(f32[1,2048]{1,0:T(1,128)} %param.17) | copy-start | bytes 24580
  7.2 0.7 %copy-start.4 = (f32[1,2048]{1,0:T(1,128)S(1)}, f32[1,2048]{1,0:T(1,128)}, u32[]{:S(2)}) copy-start(f32[1,2048]{1,0:T(1,128)} %param.18) | copy-start | bytes 24580
  7.9 0.7 %copy-start.5 = (f32[1,2048]{1,0:T(1,128)S(1)}, f32[1,2048]{1,0:T(1,128)}, u32[]{:S(2)}) copy-start(f32[1,2048]{1,0:T(1,128)} %param.19) | copy-start | bytes 24580
  8.6 0.7 copy-start.6

commit v2 on v1

--- a/solution.py
+++ b/solution.py
@@ -14,6 +14,7 @@
 Z_LEN = 32
 CHUNK = 256
 LOADS = 4
+VMEM_BYTES = 60 * 1024 * 1024
 
 EXCHANGE_COEF = 0.98
 HARTREE_SCALE = 0.5
@@ -59,13 +60,14 @@
 
 def kernel(
     sizes,
+    ids_hbm, extra_hbm, count_hbm, live_hbm,
+    basis_hbm, density_hbm, core_hbm, weight_hbm, pos_hbm, ext_hbm,
+    ham_hbm, pot_hbm,
     ids_ref, extra_ref, count_ref, live_ref,
-    basis_hbm, density_hbm, core_hbm, weight_hbm, pos_hbm, ext_hbm,
-    ham_ref, pot_ref,
     basis, left, flipped, tiles, arrived, core_row, weight_row, pos_row, ext_row,
     acc, rho_own, rho_slots, mom_row, mom_slots, part_row, part_slots,
-    weighted, quad, lent, returned,
-    load_sem, small_sem, den_sem, rho_sem, mom_sem, part_sem, lent_sem,
+    weighted, quad, lent, returned, ham_ref, pot_ref,
+    load_sem, small_sem, index_sem, den_sem, rho_sem, mom_sem, part_sem, lent_sem, out_sem,
 ):
     groups, members, z_len, points = sizes
     x_len = groups // z_len
@@ -110,6 +112,19 @@
         )
     ]
 
+    g_up = lax.rem(g + 1, groups)
+    tiny = [
+        pltpu.make_async_copy(src, dst, index_sem.at[i])
+        for i, (src, dst) in enumerate(
+            [
+                (ids_hbm, ids_ref),
+                (extra_hbm, extra_ref),
+                (count_hbm, count_ref),
+                (live_hbm, live_ref),
+            ]
+        )
+    ]
+
     barrier = pltpu.get_barrier_semaphore()
     for neighbour in (up, down):
         pl.semaphore_signal(barrier, inc=1, device_id=neighbour, device_id_type=MESH)
@@ -124,23 +139,26 @@
 
     lax.fori_loop(1, z_len, greet_z, 0)
     lax.fori_loop(1, plane, greet_plane, 0)
+    for copy in tiny:
+        copy.start()
     small[0].start()
     for copy in loads:
         copy.start()
     for copy in small[1:]:
         copy.start()
 
+    for copy in tiny:
+        copy.wait()
     extra_list = [extra_ref[0, slot] for slot in range(NXT)]
-    extra_num = count_ref[0]
-    g_up = lax.rem(g + 1, groups)
+    extra_num = count_ref[0, 0]
     own_places = [
         (place_inner if s < inner_slots else place_cross)(
-            ids_ref[g, m * owned + s], extra_list, extra_num
+            ids_ref[m * owned + s, g], extra_list, extra_num
         )
         for s in range(owned)
     ]
     next_places = [
-        place_next(ids_ref[g_up, m * owned + s], extra_list, extra_num)
+        place_next(ids_ref[m * owned + s, g_up], extra_list, extra_num)
         for s in range(inner_slots)
     ]
 
@@ -178,13 +196,8 @@
 
     for i in range(LOADS):
         loads[i].wait()
-
-    def own_chunk(c, carry):
-        span = pl.ds(pl.multiple_of(c * CHUNK, CHUNK), CHUNK)
+        span = slice(i * part, (i + 1) * part)
         acc[span, :] = tile_terms(span, tiles, range(owned))
-        return carry
-
-    lax.fori_loop(0, points // CHUNK, own_chunk, 0)
     for copy in small[1:]:
         copy.wait()
 
@@ -193,22 +206,20 @@
         factor = next_places[s][3].astype(F32)
         arrived[s] = (arrived[s].astype(F32) * factor).astype(BF16)
 
-    def next_chunk(c, carry):
-        span = pl.ds(pl.multiple_of(c * CHUNK, CHUNK), CHUNK)
+    for c in range(points // CHUNK):
+        span = slice(c * CHUNK, (c + 1) * CHUNK)
         total = acc[span, :] + tile_terms(span, arrived, range(owned, len(places)))
         for i in range(CHUNK // NB):
             turned = total[i * NB : (i + 1) * NB].T
-            rho_own[pl.ds(c * (CHUNK // NB) + i, 1), :] = jnp.sum(turned, axis=0, keepdims=True)
-        return carry
-
-    lax.fori_loop(0, points // CHUNK, next_chunk, 0)
+            at = c * (CHUNK // NB) + i
+            rho_own[at : at + 1, :] = jnp.sum(turned, axis=0, keepdims=True)
 
     rho_part = rho_own[...]
     pos = pos_row[...]
     index = lax.broadcasted_iota(jnp.int32, (rows, NB), 0) * NB + lax.broadcasted_iota(
         jnp.int32, (rows, NB), 1
     )
-    live = jnp.where(index < live_ref[0], F32(1.0), F32(0.0))
+    live = jnp.where(index < live_ref[0, 0], F32(1.0), F32(0.0))
     live_weight = weight_row[...] * live
     core_share = jnp.where(m == 0, F32(1.0), F32(0.0))
     term = live_weight * (rho_part + core_row[...] * core_share) * F32(1.0 / (groups * points))
@@ -323,6 +334,8 @@
         far = far * pos + moments[power]
     potential = local + F32(HARTREE_SCALE) * far
     pot_ref[...] = potential
+    pot_out = pltpu.make_async_copy(pot_ref, pot_hbm, out_sem.at[owned])
+    pot_out.start()
     quad[...] = scaled_weight * potential
 
     def ham_tile(s):
@@ -346,11 +359,19 @@
         )
         copy.start()
         lent_copies.append(copy)
+    ham_out = [
+        pltpu.make_async_copy(ham_ref.at[s], ham_hbm.at[s], out_sem.at[s]) for s in range(owned)
+    ]
     for s in range(owned):
         ham_ref[s] = ham_tile(s)
+        if s >= inner_slots:
+            ham_out[s].start()
     for s in range(inner_slots):
         lent_copies[s].wait()
         ham_ref[s] = ham_ref[s] + returned[s]
+        ham_out[s].start()
+    for copy in ham_out + [pot_out]:
+        copy.wait()
 
     mom_all.wait_send()
     rho_all.wait_send()
@@ -370,18 +391,20 @@
     columns = basis_values.shape[2]
     z_len = min(Z_LEN, groups)
     plane = groups // z_len * members
-    smem = pl.BlockSpec(memory_space=pltpu.SMEM)
-    anywhere = pl.BlockSpec(memory_space=pl.ANY)
-    vmem = pl.BlockSpec(memory_space=pltpu.VMEM)
+    hbm = pl.BlockSpec(memory_space=pltpu.HBM)
     ham_tiles, potential = pl.pallas_call(
         functools.partial(kernel, (groups, members, z_len, points)),
         out_shape=(
             jax.ShapeDtypeStruct((owned, NB, NB), F32),
             jax.ShapeDtypeStruct((rows, NB), F32),
         ),
-        in_specs=[smem] * 4 + [anywhere] * 6,
-        out_specs=(vmem, vmem),
+        in_specs=[hbm] * 10,
+        out_specs=(hbm, hbm),
         scratch_shapes=[
+            pltpu.SMEM((members * owned, groups), jnp.int32),
+            pltpu.SMEM((1, NXT), jnp.int32),
+            pltpu.SMEM((1, 1), jnp.int32),
+            pltpu.SMEM((1, 1), jnp.int32),
             pltpu.VMEM((points, columns), BF16),
             pltpu.VMEM((owned + inner_slots, points, NB), BF16),
             pltpu.VMEM((owned + inner_slots, NB, points), BF16),
@@ -402,20 +425,24 @@
             pltpu.VMEM((rows, NB), F32),
             pltpu.VMEM((inner_slots, NB, NB), F32),
             pltpu.VMEM((inner_slots, NB, NB), F32),
+            pltpu.VMEM((owned, NB, NB), F32),
+            pltpu.VMEM((rows, NB), F32),
             pltpu.SemaphoreType.DMA((LOADS,)),
             pltpu.SemaphoreType.DMA((5,)),
+            pltpu.SemaphoreType.DMA((4,)),
             pltpu.SemaphoreType.DMA((2,)),
             pltpu.SemaphoreType.DMA((2,)),
             pltpu.SemaphoreType.DMA((2,)),
             pltpu.SemaphoreType.DMA((2,)),
             pltpu.SemaphoreType.DMA((2, inner_slots)),
+            pltpu.SemaphoreType.DMA((owned + 1,)),
         ],
         compiler_params=pltpu.CompilerParams(
-            collective_id=0, has_side_effects=True, vmem_limit_bytes=40 * 1024 * 1024
+            collective_id=0, has_side_effects=True, vmem_limit_bytes=VMEM_BYTES
         ),
         name="density_hamiltonian",
     )(
-        tile_ids, extra_blocks, extra_count, point_count,
+        tile_ids.T, extra_blocks, extra_count.reshape(1, 1), point_count.reshape(1, 1),
         basis_values, density,
         core_density.reshape(rows, NB), grid_weights.reshape(rows, NB),
         point_pos.reshape(rows, NB), external.reshape(rows, NB),

time: 70 us -> 62.1 us (0.89)
  local copies, waits for them, and re-layouts: 8.65 us -> 2.97 us
  Pallas kernels: 58.9 us -> 57 us
    unnamed x17 -> x2, local copies, waits for them, and re-layouts: 8.65 us -> 2.97 us
    pallas_call x1, Pallas kernels: 58.9 us -> 57 us  [body(): pl.pallas_call(functools.partial(kernel, (groups, members, z_len, points)...]
where the time goes in v2:
time: 62.1 us; the launch traced here: 61.9 us
  Pallas kernels  57 us (92%)
  local copies, waits for them, and re-layouts  2.97 us (5%)
  between operations  1.93 us (3%)
    pallas_call x1, Pallas kernels, body(): pl.pallas_call(functools.partial(kernel, (groups, members, z_len, points)...  57 us
    unnamed x2, local copies, waits for them, and re-layouts  2.97 us

profile of v2, /device:TPU:1, one launch (start us, length us, event | category | flops | bytes accessed | tf_op | source)
XLA Modules:
  0.0 61.9 jit_solution(17978119620295813298)
XLA Ops:
  1.9 57.0 %density_hamiltonian.1 = (f32[4,128,128]{2,1,0:T(8,128)}, f32[16,128]{1,0:T(8,128)}) custom-call(s32[32,128]{1,0:T(8,128)} %bitcast.10, s32[1,4]{1,0:T(1,128)} %extra_hbm.1, s32[1,1]{1,0:T(1,128)} %bitcast.8.count_hbm, s32[1,1]{1,0:T(1,128)} %bitcast.9.live_hbm, bf16[1,2048,1024]{2,1,0:T(8,128)(2,1)} %basis_hbm.1, bf16[4,128,128]{2,1,0:T(8,128)(2,1)} %density_hbm.1, ...), custom_call_target="tpu_custom_call" | custom-call | tf_op jit(solution)/shard_map/density_hamiltonian/pallas_call | solution.py:395
  58.9 1.7 %copy.16 = f32[4,128,128]{2,1,0:T(8,128)} copy(f32[4,128,128]{2,1,0:T(8,128)} %get-tuple-element.8) | data formatting | bytes 524288
  60.6 1.3 %copy.17 = f32[1,2048]{1,0:T(1,128)} copy(f32[1,2048]{1,0:T(1,128)} %bitcast.15) | data formatting | bytes 16384

commit v3 on v2

--- a/solution.py
+++ b/solution.py
@@ -62,11 +62,11 @@
     sizes,
     ids_hbm, extra_hbm, count_hbm, live_hbm,
     basis_hbm, density_hbm, core_hbm, weight_hbm, pos_hbm, ext_hbm,
-    ham_hbm, pot_hbm,
+    ham_hbm, returned, pot_hbm,
     ids_ref, extra_ref, count_ref, live_ref,
     basis, left, flipped, tiles, arrived, core_row, weight_row, pos_row, ext_row,
     acc, rho_own, rho_slots, mom_row, mom_slots, part_row, part_slots,
-    weighted, quad, lent, returned, ham_ref, pot_ref,
+    weighted, quad, lent, ham_ref, pot_ref,
     load_sem, small_sem, index_sem, den_sem, rho_sem, mom_sem, part_sem, lent_sem, out_sem,
 ):
     groups, members, z_len, points = sizes
@@ -272,14 +272,6 @@
 
     lax.fori_loop(1, members, send_rho, 0)
 
-    def flip_chunk(c, carry):
-        span = pl.ds(pl.multiple_of(c * NB, NB), NB)
-        for s, (_, _, col, _) in enumerate(places):
-            flipped[s, :, span] = pick(basis, span, firsts[s][1], col).T
-        return carry
-
-    lax.fori_loop(0, rows, flip_chunk, 0)
-
     def wait_all(slots, count, sem, target):
         both = pltpu.make_async_remote_copy(
             src_ref=slots.at[pl.ds(0, count)],
@@ -312,6 +304,14 @@
         return carry
 
     lax.fori_loop(1, plane, send_part, 0)
+
+    def flip_chunk(c, carry):
+        span = pl.ds(pl.multiple_of(c * NB, NB), NB)
+        for s, (_, _, col, _) in enumerate(places):
+            flipped[s, :, span] = pick(basis, span, firsts[s][1], col).T
+        return carry
+
+    lax.fori_loop(0, rows, flip_chunk, 0)
 
     rho_all = wait_all(rho_slots, members - 1, rho_sem, in_group(1))
     rho_all.wait_recv()
@@ -364,18 +364,39 @@
     ]
     for s in range(owned):
         ham_ref[s] = ham_tile(s)
-        if s >= inner_slots:
-            ham_out[s].start()
-    for s in range(inner_slots):
-        lent_copies[s].wait()
-        ham_ref[s] = ham_ref[s] + returned[s]
         ham_out[s].start()
-    for copy in ham_out + [pot_out]:
+    for copy in ham_out + [pot_out] + lent_copies:
         copy.wait()
 
     mom_all.wait_send()
     rho_all.wait_send()
     part_all.wait_send()
+
+
+def finish(own_hbm, returned_hbm, pot_in, ham_hbm, pot_hbm, own, lent, pot, sem):
+    inner_slots = returned_hbm.shape[0]
+    first = pl.ds(0, inner_slots)
+    others = pl.ds(inner_slots, own_hbm.shape[0] - inner_slots)
+    copy = pltpu.make_async_copy
+    load_first = copy(own_hbm.at[first], own.at[first], sem.at[0])
+    load_lent = copy(returned_hbm, lent, sem.at[1])
+    load_others = copy(own_hbm.at[others], own.at[others], sem.at[2])
+    load_pot = copy(pot_in, pot, sem.at[3])
+    for load in (load_first, load_lent, load_others, load_pot):
+        load.start()
+    load_first.wait()
+    load_lent.wait()
+    own[first] = own[first] + lent[...]
+    store_first = copy(own.at[first], ham_hbm.at[first], sem.at[4])
+    store_first.start()
+    load_others.wait()
+    store_others = copy(own.at[others], ham_hbm.at[others], sem.at[5])
+    store_others.start()
+    load_pot.wait()
+    store_pot = copy(pot, pot_hbm, sem.at[6])
+    store_pot.start()
+    for store in (store_first, store_others, store_pot):
+        store.wait()
 
 
 def body(
@@ -392,14 +413,15 @@
     z_len = min(Z_LEN, groups)
     plane = groups // z_len * members
     hbm = pl.BlockSpec(memory_space=pltpu.HBM)
-    ham_tiles, potential = pl.pallas_call(
+    own_ham, returned, potential = pl.pallas_call(
         functools.partial(kernel, (groups, members, z_len, points)),
         out_shape=(
             jax.ShapeDtypeStruct((owned, NB, NB), F32),
+            jax.ShapeDtypeStruct((inner_slots, NB, NB), F32),
             jax.ShapeDtypeStruct((rows, NB), F32),
         ),
         in_specs=[hbm] * 10,
-        out_specs=(hbm, hbm),
+        out_specs=(hbm, hbm, hbm),
         scratch_shapes=[
             pltpu.SMEM((members * owned, groups), jnp.int32),
             pltpu.SMEM((1, NXT), jnp.int32),
@@ -423,7 +445,6 @@
             pltpu.VMEM((plane, 1, NB), F32),
             pltpu.VMEM((NB, points), BF16),
             pltpu.VMEM((rows, NB), F32),
-            pltpu.VMEM((inner_slots, NB, NB), F32),
             pltpu.VMEM((inner_slots, NB, NB), F32),
             pltpu.VMEM((owned, NB, NB), F32),
             pltpu.VMEM((rows, NB), F32),
@@ -447,6 +468,23 @@
         core_density.reshape(rows, NB), grid_weights.reshape(rows, NB),
         point_pos.reshape(rows, NB), external.reshape(rows, NB),
     )
+    ham_tiles, potential = pl.pallas_call(
+        finish,
+        out_shape=(
+            jax.ShapeDtypeStruct((owned, NB, NB), F32),
+            jax.ShapeDtypeStruct((rows, NB), F32),
+        ),
+        in_specs=[hbm] * 3,
+        out_specs=(hbm, hbm),
+        scratch_shapes=[
+            pltpu.VMEM((owned, NB, NB), F32),
+            pltpu.VMEM((inner_slots, NB, NB), F32),
+            pltpu.VMEM((rows, NB), F32),
+            pltpu.SemaphoreType.DMA((7,)),
+        ],
+        compiler_params=pltpu.CompilerParams(vmem_limit_bytes=VMEM_BYTES),
+        name="finish",
+    )(own_ham, returned, potential)
     return ham_tiles, potential.reshape(1, points)
 
 

time: 62.1 us -> 60.3 us (0.971)
  local copies, waits for them, and re-layouts: 2.97 us -> 0 us
  Pallas kernels: 57 us -> 58.2 us
    unnamed x2 -> x0, local copies, waits for them, and re-layouts: 2.97 us -> none
    pallas_call x0 -> x1, Pallas kernels: none -> 1.75 us  [body(): pl.pallas_call(finish, out_shape=(jax.ShapeDtypeStruct((owned, NB, NB), F...]
where the time goes in v3:
time: 60.3 us; the launch traced here: 60.1 us
  Pallas kernels  58.2 us (97%)
  between operations  1.93 us (3%)
    pallas_call x1, Pallas kernels, body(): pl.pallas_call(functools.partial(kernel, (groups, members, z_len, points)...  56.5 us
    pallas_call x1, Pallas kernels, body(): pl.pallas_call(finish, out_shape=(jax.ShapeDtypeStruct((owned, NB, NB), F...  1.75 us

profile of v3, /device:TPU:1, one launch (start us, length us, event | category | flops | bytes accessed | tf_op | source)
XLA Modules:
  0.0 60.1 jit_solution(8171333225320080291)
XLA Ops:
  1.9 56.5 %density_hamiltonian.1 = (f32[4,128,128]{2,1,0:T(8,128)}, f32[2,128,128]{2,1,0:T(8,128)}, f32[16,128]{1,0:T(8,128)}) custom-call(s32[32,128]{1,0:T(8,128)} %bitcast.10, s32[1,4]{1,0:T(1,128)} %extra_hbm.1, s32[1,1]{1,0:T(1,128)} %bitcast.8.count_hbm, s32[1,1]{1,0:T(1,128)} %bitcast.9.live_hbm, bf16[1,2048,1024]{2,1,0:T(8,128)(2,1)} %basis_hbm.1, ...), custom_call_target="tpu_custom_call" | custom-call | tf_op jit(solution)/shard_map/density_hamiltonian/pallas_call | solution.py:416
  58.4 1.7 %finish.1 = (f32[4,128,128]{2,1,0:T(8,128)}, f32[16,128]{1,0:T(8,128)}) custom-call(f32[4,128,128]{2,1,0:T(8,128)} %get-tuple-element.7.own_hbm, f32[2,128,128]{2,1,0:T(8,128)} %get-tuple-element.8.returned_hbm, f32[16,128]{1,0:T(8,128)} %get-tuple-element.9.pot_in), custom_call_target="tpu_custom_call" | custom-call | tf_op jit(solution)/shard_map/finish/pallas_call | solution.py:471

commit v4 on v3

--- a/solution.py
+++ b/solution.py
@@ -84,6 +84,13 @@
     up = (lax.rem(g + 1, groups), m)
     down = (lax.rem(g + groups - 1, groups), m)
 
+    def far_z(i):
+        return z_len // 2 + lax.div(i + 1, 2) * (1 - 2 * lax.rem(i, 2))
+
+    def far_plane(i):
+        first = plane // 2 + members - 2
+        return lax.rem(first + (plane - 1) - i, plane - 1) + 1
+
     def along_z(step):
         return (x * z_len + lax.rem(z + step, z_len), m)
 
@@ -129,24 +136,26 @@
     for neighbour in (up, down):
         pl.semaphore_signal(barrier, inc=1, device_id=neighbour, device_id_type=MESH)
 
-    def greet_plane(step, carry):
-        pl.semaphore_signal(barrier, inc=1, device_id=in_plane(step), device_id_type=MESH)
-        return carry
-
-    def greet_z(step, carry):
-        pl.semaphore_signal(barrier, inc=1, device_id=along_z(step), device_id_type=MESH)
-        return carry
-
-    lax.fori_loop(1, z_len, greet_z, 0)
-    lax.fori_loop(1, plane, greet_plane, 0)
+    small[0].start()
     for copy in tiny:
         copy.start()
-    small[0].start()
     for copy in loads:
         copy.start()
     for copy in small[1:]:
         copy.start()
 
+    def greet_z(i, carry):
+        there = along_z(far_z(i))
+        pl.semaphore_signal(barrier, inc=1, device_id=there, device_id_type=MESH)
+        return carry
+
+    def greet_plane(i, carry):
+        there = in_plane(far_plane(i))
+        pl.semaphore_signal(barrier, inc=1, device_id=there, device_id_type=MESH)
+        return carry
+
+    lax.fori_loop(0, z_len - 1, greet_z, 0, unroll=True)
+    lax.fori_loop(0, plane - 1, greet_plane, 0, unroll=True)
     for copy in tiny:
         copy.wait()
     extra_list = [extra_ref[0, slot] for slot in range(NXT)]
@@ -248,11 +257,10 @@
         )
 
     def send_mom(i, carry):
-        step = z_len // 2 + lax.div(i + 1, 2) * (1 - 2 * lax.rem(i, 2))
-        mom_copy(step).start()
+        mom_copy(far_z(i)).start()
         return carry
 
-    lax.fori_loop(0, z_len - 1, send_mom, 0)
+    lax.fori_loop(0, z_len - 1, send_mom, 0, unroll=True)
 
     rho_slots[m] = rho_part
 
@@ -270,7 +278,7 @@
         rho_copy(step).start()
         return carry
 
-    lax.fori_loop(1, members, send_rho, 0)
+    lax.fori_loop(1, members, send_rho, 0, unroll=True)
 
     def wait_all(slots, count, sem, target):
         both = pltpu.make_async_remote_copy(
@@ -299,11 +307,11 @@
             device_id_type=MESH,
         )
 
-    def send_part(step, carry):
-        part_copy(step).start()
+    def send_part(i, carry):
+        part_copy(far_plane(i)).start()
         return carry
 
-    lax.fori_loop(1, plane, send_part, 0)
+    lax.fori_loop(0, plane - 1, send_part, 0, unroll=True)
 
     def flip_chunk(c, carry):
         span = pl.ds(pl.multiple_of(c * NB, NB), NB)
@@ -357,16 +365,19 @@
             device_id=up,
             device_id_type=MESH,
         )
-        copy.start()
         lent_copies.append(copy)
+        pl.when(g < groups - 1)(copy.start)
     ham_out = [
         pltpu.make_async_copy(ham_ref.at[s], ham_hbm.at[s], out_sem.at[s]) for s in range(owned)
     ]
     for s in range(owned):
         ham_ref[s] = ham_tile(s)
         ham_out[s].start()
-    for copy in ham_out + [pot_out] + lent_copies:
+    for copy in ham_out + [pot_out]:
         copy.wait()
+    for copy in lent_copies:
+        pl.when(g < groups - 1)(copy.wait_send)
+        pl.when(g > 0)(copy.wait_recv)
 
     mom_all.wait_send()
     rho_all.wait_send()
@@ -386,7 +397,8 @@
         load.start()
     load_first.wait()
     load_lent.wait()
-    own[first] = own[first] + lent[...]
+    below = lax.axis_index("batch") > 0
+    own[first] = own[first] + jnp.where(below, lent[...], F32(0.0))
     store_first = copy(own.at[first], ham_hbm.at[first], sem.at[4])
     store_first.start()
     load_others.wait()

time: 60.3 us -> 59 us (0.978)
  the two profiles are of different devices: /device:TPU:1 before, /device:TPU:2 now
where the time goes in v4:
time: 59 us; the launch traced here: 58.8 us
  Pallas kernels  56.9 us (96%)
  between operations  1.93 us (3%)
    pallas_call x1, Pallas kernels, body(): pl.pallas_call(functools.partial(kernel, (groups, members, z_len, points)...  55.1 us
    pallas_call x1, Pallas kernels, body(): pl.pallas_call(finish, out_shape=(jax.ShapeDtypeStruct((owned, NB, NB), F...  1.75 us

profile of v4, /device:TPU:2, one launch (start us, length us, event | category | flops | bytes accessed | tf_op | source)
XLA Modules:
  0.0 58.8 jit_solution(9723260541784748816)
XLA Ops:
  1.9 55.1 %density_hamiltonian.1 = (f32[4,128,128]{2,1,0:T(8,128)}, f32[2,128,128]{2,1,0:T(8,128)}, f32[16,128]{1,0:T(8,128)}) custom-call(s32[32,128]{1,0:T(8,128)} %bitcast.10, s32[1,4]{1,0:T(1,128)} %extra_hbm.1, s32[1,1]{1,0:T(1,128)} %bitcast.8.count_hbm, s32[1,1]{1,0:T(1,128)} %bitcast.9.live_hbm, bf16[1,2048,1024]{2,1,0:T(8,128)(2,1)} %basis_hbm.1, ...), custom_call_target="tpu_custom_call" | custom-call | tf_op jit(solution)/shard_map/density_hamiltonian/pallas_call | solution.py:428
  57.1 1.7 %finish.1 = (f32[4,128,128]{2,1,0:T(8,128)}, f32[16,128]{1,0:T(8,128)}) custom-call(f32[4,128,128]{2,1,0:T(8,128)} %get-tuple-element.7.own_hbm, f32[2,128,128]{2,1,0:T(8,128)} %get-tuple-element.8.returned_hbm, f32[16,128]{1,0:T(8,128)} %get-tuple-element.9.pot_in), custom_call_target="tpu_custom_call" | custom-call | tf_op jit(solution)/shard_map/finish/pallas_call | solution.py:483

commit v5 on v4

--- a/solution.py
+++ b/solution.py
@@ -173,15 +173,19 @@
 
     pl.semaphore_wait(barrier, (z_len - 1) + (plane - 1) + 2)
 
-    density_copy = pltpu.make_async_remote_copy(
-        src_ref=density_hbm.at[pl.ds(0, inner_slots)],
-        dst_ref=arrived,
-        send_sem=den_sem.at[0],
-        recv_sem=den_sem.at[1],
-        device_id=down,
-        device_id_type=MESH,
-    )
-    density_copy.start()
+    density_copies = [
+        pltpu.make_async_remote_copy(
+            src_ref=density_hbm.at[s],
+            dst_ref=arrived.at[s],
+            send_sem=den_sem.at[0, s],
+            recv_sem=den_sem.at[1, s],
+            device_id=down,
+            device_id_type=MESH,
+        )
+        for s in range(inner_slots)
+    ]
+    for copy in density_copies:
+        copy.start()
 
     small[0].wait()
     for s in range(owned):
@@ -210,18 +214,20 @@
     for copy in small[1:]:
         copy.wait()
 
-    density_copy.wait()
     for s in range(inner_slots):
+        density_copies[s].wait()
         factor = next_places[s][3].astype(F32)
         arrived[s] = (arrived[s].astype(F32) * factor).astype(BF16)
-
-    for c in range(points // CHUNK):
-        span = slice(c * CHUNK, (c + 1) * CHUNK)
-        total = acc[span, :] + tile_terms(span, arrived, range(owned, len(places)))
-        for i in range(CHUNK // NB):
-            turned = total[i * NB : (i + 1) * NB].T
-            at = c * (CHUNK // NB) + i
-            rho_own[at : at + 1, :] = jnp.sum(turned, axis=0, keepdims=True)
+        for c in range(points // CHUNK):
+            span = slice(c * CHUNK, (c + 1) * CHUNK)
+            total = acc[span, :] + tile_terms(span, arrived.at[pl.ds(s, 1)], [owned + s])
+            if s < inner_slots - 1:
+                acc[span, :] = total
+                continue
+            for i in range(CHUNK // NB):
+                turned = total[i * NB : (i + 1) * NB].T
+                at = c * (CHUNK // NB) + i
+                rho_own[at : at + 1, :] = jnp.sum(turned, axis=0, keepdims=True)
 
     rho_part = rho_own[...]
     pos = pos_row[...]
@@ -386,29 +392,29 @@
 
 def finish(own_hbm, returned_hbm, pot_in, ham_hbm, pot_hbm, own, lent, pot, sem):
     inner_slots = returned_hbm.shape[0]
-    first = pl.ds(0, inner_slots)
-    others = pl.ds(inner_slots, own_hbm.shape[0] - inner_slots)
+    owned = own_hbm.shape[0]
     copy = pltpu.make_async_copy
-    load_first = copy(own_hbm.at[first], own.at[first], sem.at[0])
-    load_lent = copy(returned_hbm, lent, sem.at[1])
-    load_others = copy(own_hbm.at[others], own.at[others], sem.at[2])
-    load_pot = copy(pot_in, pot, sem.at[3])
-    for load in (load_first, load_lent, load_others, load_pot):
+    load_own = [copy(own_hbm.at[s], own.at[s], sem.at[0, s]) for s in range(owned)]
+    load_lent = [copy(returned_hbm.at[s], lent.at[s], sem.at[1, s]) for s in range(inner_slots)]
+    store = [copy(own.at[s], ham_hbm.at[s], sem.at[2, s]) for s in range(owned)]
+    load_pot = copy(pot_in, pot, sem.at[1, inner_slots])
+    store_pot = copy(pot, pot_hbm, sem.at[1, inner_slots + 1])
+    for s in range(inner_slots):
+        load_lent[s].start()
+        load_own[s].start()
+    for load in load_own[inner_slots:] + [load_pot]:
         load.start()
-    load_first.wait()
-    load_lent.wait()
     below = lax.axis_index("batch") > 0
-    own[first] = own[first] + jnp.where(below, lent[...], F32(0.0))
-    store_first = copy(own.at[first], ham_hbm.at[first], sem.at[4])
-    store_first.start()
-    load_others.wait()
-    store_others = copy(own.at[others], ham_hbm.at[others], sem.at[5])
-    store_others.start()
+    for s in range(owned):
+        load_own[s].wait()
+        if s < inner_slots:
+            load_lent[s].wait()
+            own[s] = own[s] + jnp.where(below, lent[s], F32(0.0))
+        store[s].start()
     load_pot.wait()
-    store_pot = copy(pot, pot_hbm, sem.at[6])
     store_pot.start()
-    for store in (store_first, store_others, store_pot):
-        store.wait()
+    for done in store + [store_pot]:
+        done.wait()
 
 
 def body(
@@ -463,7 +469,7 @@
             pltpu.SemaphoreType.DMA((LOADS,)),
             pltpu.SemaphoreType.DMA((5,)),
             pltpu.SemaphoreType.DMA((4,)),
-            pltpu.SemaphoreType.DMA((2,)),
+            pltpu.SemaphoreType.DMA((2, inner_slots)),
             pltpu.SemaphoreType.DMA((2,)),
             pltpu.SemaphoreType.DMA((2,)),
             pltpu.SemaphoreType.DMA((2,)),
@@ -492,7 +498,7 @@
             pltpu.VMEM((owned, NB, NB), F32),
             pltpu.VMEM((inner_slots, NB, NB), F32),
             pltpu.VMEM((rows, NB), F32),
-            pltpu.SemaphoreType.DMA((7,)),
+            pltpu.SemaphoreType.DMA((3, owned)),
         ],
         compiler_params=pltpu.CompilerParams(vmem_limit_bytes=VMEM_BYTES),
         name="finish",

time: 59 us -> 58.9 us (level)
  no operation moved by 1% of the time
where the time goes in v5:
time: 58.9 us; the launch traced here: 58.7 us
  Pallas kernels  56.7 us (96%)
  between operations  1.93 us (3%)
    pallas_call x1, Pallas kernels, body(): pl.pallas_call(functools.partial(kernel, (groups, members, z_len, points)...  55 us
    pallas_call x1, Pallas kernels, body(): pl.pallas_call(finish, out_shape=(jax.ShapeDtypeStruct((owned, NB, NB), F...  1.73 us

profile of v5, /device:TPU:2, one launch (start us, length us, event | category | flops | bytes accessed | tf_op | source)
XLA Modules:
  0.0 58.7 jit_solution(3923022874235673296)
XLA Ops:
  1.9 55.0 %density_hamiltonian.1 = (f32[4,128,128]{2,1,0:T(8,128)}, f32[2,128,128]{2,1,0:T(8,128)}, f32[16,128]{1,0:T(8,128)}) custom-call(s32[32,128]{1,0:T(8,128)} %bitcast.10, s32[1,4]{1,0:T(1,128)} %extra_hbm.1, s32[1,1]{1,0:T(1,128)} %bitcast.8.count_hbm, s32[1,1]{1,0:T(1,128)} %bitcast.9.live_hbm, bf16[1,2048,1024]{2,1,0:T(8,128)(2,1)} %basis_hbm.1, ...), custom_call_target="tpu_custom_call" | custom-call | tf_op jit(solution)/shard_map/density_hamiltonian/pallas_call | solution.py:434
  56.9 1.7 %finish.1 = (f32[4,128,128]{2,1,0:T(8,128)}, f32[16,128]{1,0:T(8,128)}) custom-call(f32[4,128,128]{2,1,0:T(8,128)} %get-tuple-element.7.own_hbm, f32[2,128,128]{2,1,0:T(8,128)} %get-tuple-element.8.returned_hbm, f32[16,128]{1,0:T(8,128)} %get-tuple-element.9.pot_in), custom_call_target="tpu_custom_call" | custom-call | tf_op jit(solution)/shard_map/finish/pallas_call | solution.py:489

commit v6 on v5

--- a/solution.py
+++ b/solution.py
@@ -86,6 +86,10 @@
 
     def far_z(i):
         return z_len // 2 + lax.div(i + 1, 2) * (1 - 2 * lax.rem(i, 2))
+
+    def in_turn(i):
+        half = lax.div(i, 2)
+        return far_z(half + lax.rem(i, 2) * (z_len - 2 - 2 * half))
 
     def far_plane(i):
         first = plane // 2 + members - 2
@@ -263,7 +267,7 @@
         )
 
     def send_mom(i, carry):
-        mom_copy(far_z(i)).start()
+        mom_copy(in_turn(i)).start()
         return carry
 
     lax.fori_loop(0, z_len - 1, send_mom, 0, unroll=True)
@@ -347,9 +351,6 @@
     for power in (2, 1, 0):
         far = far * pos + moments[power]
     potential = local + F32(HARTREE_SCALE) * far
-    pot_ref[...] = potential
-    pot_out = pltpu.make_async_copy(pot_ref, pot_hbm, out_sem.at[owned])
-    pot_out.start()
     quad[...] = scaled_weight * potential
 
     def ham_tile(s):
@@ -373,6 +374,9 @@
         )
         lent_copies.append(copy)
         pl.when(g < groups - 1)(copy.start)
+    pot_ref[...] = potential
+    pot_out = pltpu.make_async_copy(pot_ref, pot_hbm, out_sem.at[owned])
+    pot_out.start()
     ham_out = [
         pltpu.make_async_copy(ham_ref.at[s], ham_hbm.at[s], out_sem.at[s]) for s in range(owned)
     ]

time: 58.9 us -> 58.9 us (level)
  no operation moved by 1% of the time
where the time goes in v6:
time: 58.9 us; the launch traced here: 58.7 us
  Pallas kernels  56.7 us (96%)
  between operations  1.93 us (3%)
    pallas_call x1, Pallas kernels, body(): pl.pallas_call(functools.partial(kernel, (groups, members, z_len, points)...  55 us
    pallas_call x1, Pallas kernels, body(): pl.pallas_call(finish, out_shape=(jax.ShapeDtypeStruct((owned, NB, NB), F...  1.73 us

profile of v6, /device:TPU:2, one launch (start us, length us, event | category | flops | bytes accessed | tf_op | source)
XLA Modules:
  0.0 58.7 jit_solution(12864495127919983071)
XLA Ops:
  1.9 55.0 %density_hamiltonian.1 = (f32[4,128,128]{2,1,0:T(8,128)}, f32[2,128,128]{2,1,0:T(8,128)}, f32[16,128]{1,0:T(8,128)}) custom-call(s32[32,128]{1,0:T(8,128)} %bitcast.10, s32[1,4]{1,0:T(1,128)} %extra_hbm.1, s32[1,1]{1,0:T(1,128)} %bitcast.8.count_hbm, s32[1,1]{1,0:T(1,128)} %bitcast.9.live_hbm, bf16[1,2048,1024]{2,1,0:T(8,128)(2,1)} %basis_hbm.1, ...), custom_call_target="tpu_custom_call" | custom-call | tf_op jit(solution)/shard_map/density_hamiltonian/pallas_call | solution.py:438
  56.9 1.7 %finish.1 = (f32[4,128,128]{2,1,0:T(8,128)}, f32[16,128]{1,0:T(8,128)}) custom-call(f32[4,128,128]{2,1,0:T(8,128)} %get-tuple-element.7.own_hbm, f32[2,128,128]{2,1,0:T(8,128)} %get-tuple-element.8.returned_hbm, f32[16,128]{1,0:T(8,128)} %get-tuple-element.9.pot_in), custom_call_target="tpu_custom_call" | custom-call | tf_op jit(solution)/shard_map/finish/pallas_call | solution.py:493

commit v7 on v6

--- a/solution.py
+++ b/solution.py
@@ -160,21 +160,6 @@
 
     lax.fori_loop(0, z_len - 1, greet_z, 0, unroll=True)
     lax.fori_loop(0, plane - 1, greet_plane, 0, unroll=True)
-    for copy in tiny:
-        copy.wait()
-    extra_list = [extra_ref[0, slot] for slot in range(NXT)]
-    extra_num = count_ref[0, 0]
-    own_places = [
-        (place_inner if s < inner_slots else place_cross)(
-            ids_ref[m * owned + s, g], extra_list, extra_num
-        )
-        for s in range(owned)
-    ]
-    next_places = [
-        place_next(ids_ref[m * owned + s, g_up], extra_list, extra_num)
-        for s in range(inner_slots)
-    ]
-
     pl.semaphore_wait(barrier, (z_len - 1) + (plane - 1) + 2)
 
     density_copies = [
@@ -190,6 +175,21 @@
     ]
     for copy in density_copies:
         copy.start()
+
+    for copy in tiny:
+        copy.wait()
+    extra_list = [extra_ref[0, slot] for slot in range(NXT)]
+    extra_num = count_ref[0, 0]
+    own_places = [
+        (place_inner if s < inner_slots else place_cross)(
+            ids_ref[m * owned + s, g], extra_list, extra_num
+        )
+        for s in range(owned)
+    ]
+    next_places = [
+        place_next(ids_ref[m * owned + s, g_up], extra_list, extra_num)
+        for s in range(inner_slots)
+    ]
 
     small[0].wait()
     for s in range(owned):
@@ -385,13 +385,12 @@
         ham_out[s].start()
     for copy in ham_out + [pot_out]:
         copy.wait()
+    mom_all.wait_send()
+    rho_all.wait_send()
+    part_all.wait_send()
     for copy in lent_copies:
         pl.when(g < groups - 1)(copy.wait_send)
         pl.when(g > 0)(copy.wait_recv)
-
-    mom_all.wait_send()
-    rho_all.wait_send()
-    part_all.wait_send()
 
 
 def finish(own_hbm, returned_hbm, pot_in, ham_hbm, pot_hbm, own, lent, pot, sem):

time: 58.9 us -> 58.9 us (level)
  no operation moved by 1% of the time
where the time goes in v7:
time: 58.9 us; the launch traced here: 58.6 us
  Pallas kernels  56.7 us (96%)
  between operations  1.93 us (3%)
    pallas_call x1, Pallas kernels, body(): pl.pallas_call(functools.partial(kernel, (groups, members, z_len, points)...  55 us
    pallas_call x1, Pallas kernels, body(): pl.pallas_call(finish, out_shape=(jax.ShapeDtypeStruct((owned, NB, NB), F...  1.73 us

profile of v7, /device:TPU:2, one launch (start us, length us, event | category | flops | bytes accessed | tf_op | source)
XLA Modules:
  0.0 58.6 jit_solution(1594514923997548724)
XLA Ops:
  1.9 55.0 %density_hamiltonian.1 = (f32[4,128,128]{2,1,0:T(8,128)}, f32[2,128,128]{2,1,0:T(8,128)}, f32[16,128]{1,0:T(8,128)}) custom-call(s32[32,128]{1,0:T(8,128)} %bitcast.10, s32[1,4]{1,0:T(1,128)} %extra_hbm.1, s32[1,1]{1,0:T(1,128)} %bitcast.8.count_hbm, s32[1,1]{1,0:T(1,128)} %bitcast.9.live_hbm, bf16[1,2048,1024]{2,1,0:T(8,128)(2,1)} %basis_hbm.1, ...), custom_call_target="tpu_custom_call" | custom-call | tf_op jit(solution)/shard_map/density_hamiltonian/pallas_call | solution.py:437
  56.9 1.7 %finish.1 = (f32[4,128,128]{2,1,0:T(8,128)}, f32[16,128]{1,0:T(8,128)}) custom-call(f32[4,128,128]{2,1,0:T(8,128)} %get-tuple-element.7.own_hbm, f32[2,128,128]{2,1,0:T(8,128)} %get-tuple-element.8.returned_hbm, f32[16,128]{1,0:T(8,128)} %get-tuple-element.9.pot_in), custom_call_target="tpu_custom_call" | custom-call | tf_op jit(solution)/shard_map/finish/pallas_call | solution.py:492
